TPU v7x, 32 devices: a whole 2x2x4 slice. The times are simulated.
32 devices in a mesh: row: 8 (over z, x), col: 4 (over y, core).
Axes of the slice: x: 2, y: 2, z: 4, core: 2. Of those that a mesh axis runs over, the one named last changes fastest.
Arguments:
- factor: float32 [8192, 8192], P('row', 'col'), may hold values from -0.24 to 0.24
- adjoint: float32 [8192, 8192], P('row', 'col'), may hold values from -6 to 6
- inverse: float32 [2, 256, 256], replicated, may hold values from -1 to 3, as said below
Outputs:
- adjoint_out: float32 [8192, 8192], P('row', 'col')
Inputs may be any that keep to these rules, and one draw needn't show every extreme that they name: Each inverse[j] is lower triangular, with every diagonal entry larger than the sum of the magnitudes of the other entries of its row.
All inputs are finite; a program needn't handle non-finite values.
Results may differ from a plain program's by a relative error of at most 0.00011.
Values sent between devices are 32-bit elements; how exact they have to be, the bound alone decides.
A program may use at most 128 MiB of HBM per device.

v0:
```python
import jax
import jax.numpy as jnp
from jax import lax
from jax.sharding import PartitionSpec as P


def broadcast(value, axis, source):
    kept = jnp.where(lax.axis_index(axis) == source, value, 0).astype(value.dtype)
    return lax.psum(kept, axis)


def product(left, right):
    return jnp.dot(left, right, precision=lax.Precision.HIGHEST, preferred_element_type=jnp.float32)


def halved_lower(matrix):
    return jnp.tril(matrix) - 0.5 * jnp.diag(jnp.diagonal(matrix))


def panel_step(factor, current, column, inverse_tile, panel_tile, row_global, col_global):
    width = inverse_tile.shape[0]
    rows_count = lax.axis_size("row")
    cols_count = lax.axis_size("col")
    owner_row = panel_tile % rows_count
    owner_col = panel_tile % cols_count
    row_start = panel_tile // rows_count * width
    col_start = panel_tile // cols_count * width
    below = (row_global > panel_tile)[:, None]
    left_mask = (col_global < panel_tile)[None, :]
    on_owner_row = lax.axis_index("row") == owner_row
    on_owner_col = lax.axis_index("col") == owner_col
    factor_column = factor[:, col_start : col_start + width]
    panel_adjoint, panel_factor = (
        broadcast(column, "col", owner_col),
        broadcast(factor_column, "col", owner_col),
    )
    offdiag = jnp.where(below, product(panel_adjoint, inverse_tile), 0.0)
    factor_row = broadcast(factor[row_start : row_start + width], "row", owner_row)
    factor_row = jnp.where(left_mask, factor_row, 0.0)
    raw_row = jnp.where(on_owner_row, current[row_start : row_start + width], 0.0)
    raw_diag = jnp.where(on_owner_row, panel_adjoint[row_start : row_start + width], 0.0)
    part_row = jnp.where(left_mask, raw_row - product(offdiag.T, factor), 0.0)
    part_diag = raw_diag - product(offdiag.T, panel_factor)
    identity = jnp.eye(width, dtype=jnp.float32)
    factor_diag = lax.linalg.triangular_solve(inverse_tile, identity, left_side=True, lower=True)
    row_total, diag_total = lax.psum((part_row, part_diag), "row")
    dprime = jnp.tril(diag_total)
    wmat = product(
        product(inverse_tile.T, halved_lower(product(factor_diag.T, dprime))), inverse_tile
    )
    sym = wmat + wmat.T
    new_row = row_total - product(sym, factor_row)
    updated = current - product(offdiag, factor_row)
    row_block = jnp.where(on_owner_row & left_mask, new_row, updated[row_start : row_start + width])
    updated = updated.at[row_start : row_start + width].set(row_block)
    new_column = jnp.where(below, offdiag, column)
    diag_block = jnp.where(
        on_owner_row, halved_lower(sym), new_column[row_start : row_start + width]
    )
    new_column = new_column.at[row_start : row_start + width].set(diag_block)
    new_column = jnp.where(on_owner_col, new_column, updated[:, col_start : col_start + width])
    updated = updated.at[:, col_start : col_start + width].set(new_column)
    return (updated, column)


def per_device(factor, adjoint, inverse):
    width = inverse.shape[-1]
    rows_count = lax.axis_size("row")
    cols_count = lax.axis_size("col")
    tile_rows = factor.shape[0] // width
    tile_cols = factor.shape[1] // width
    total_tiles = tile_rows * rows_count
    first_tile = total_tiles // 2
    second_tile = first_tile - 1
    row_global = jnp.repeat(jnp.arange(tile_rows) * rows_count + lax.axis_index("row"), width)
    col_global = jnp.repeat(jnp.arange(tile_cols) * cols_count + lax.axis_index("col"), width)
    first_start = first_tile // cols_count * width
    second_start = second_tile // cols_count * width
    current, unused = panel_step(
        factor,
        adjoint,
        adjoint[:, first_start : first_start + width],
        inverse[0],
        first_tile,
        row_global,
        col_global,
    )
    current, unused = panel_step(
        factor,
        current,
        current[:, second_start : second_start + width],
        inverse[1],
        second_tile,
        row_global,
        col_global,
    )
    return current


def solution(mesh):
    return jax.shard_map(
        per_device,
        mesh=mesh,
        in_specs=(P("row", "col"), P("row", "col"), P()),
        out_specs=P("row", "col"),
        check_vma=False,
    )
```

profile of v0, /device:TPU:0, one launch (start us, length us, event | category | flops | bytes accessed | tf_op | source)
XLA Modules:
  0.0 553.9 jit_solution(4621701198111508362)
XLA Ops:
  6.5 3.8 slice_select_fusion.3
  10.6 4.9 slice_select_fusion.1
  15.5 49.3 %all-reduce.15.cloned.1.call-done = (f32[1024,256]{1,0:T(8,128)}, f32[1024,256]{1,0:T(8,128)}) async-done(((f32[1024,256]{1,0:T(8,128)}, f32[1024,256]{1,0:T(8,128)}), (f32[1024,256]{1,0:T(8,128)}, f32[1024,256]{1,0:T(8,128)})) %all-reduce.15.cloned.1.call-update) | async-done | bytes 2097168 | tf_op jit(solution)/shard_map/psum | solution.py:9
  64.8 2.6 slice_select_fusion.7
  67.4 3.5 convolution_subtract_fusion.7
  71.0 11.0 %fusion.5 = f32[256,2048]{1,0:T(8,128)} fusion(f32[1024,256]{1,0:T(8,128)S(1)} %get-tuple-element.131, f32[1024,2048]{1,0:T(8,128)} %param.17, f32[1024,2048]{1,0:T(8,128)} %param.18, pred[]{:T(512)S(6)} %eq.38, pred[2048]{0:T(1024)(128)(4,1)S(1)} %lt.46), kind=kOutput, calls=%fused_computation.19 | convolution fusion | flops 6444023808 | bytes 13633537 | tf_op jit(solution)/shard_map/dot_general | solution.py:13
  82.2 0.7 bitcast_select_fusion
  83.1 3.7 while.10
  83.1 0.6 fusion.113
  83.6 1.3 bitcast_dynamic-update-slice_fusion.4
  85.5 1.3 bitcast_dynamic-update-slice_fusion.4
  86.8 19.7 %custom-call.12 = f32[2,128,128]{1,2,0:T(8,128)S(1)} custom-call(f32[2,128,128]{2,1,0:T(8,128)S(1)} %get-tuple-element.92), custom_call_target="InvertDiagBlocksLowerTriangular" | custom-call | tf_op jit(solution)/shard_map/triangular_solve/custom-call.1 | solution.py:45
  106.5 0.7 compare_reduce_fusion.1
  108.1 138.0 %all-reduce.11.cloned.1.call-done = (f32[256,2048]{1,0:T(8,128)}, f32[256,2048]{1,0:T(8,128)}, f32[256,256]{1,0:T(8,128)}) async-done(((f32[256,2048]{1,0:T(8,128)}, f32[256,2048]{1,0:T(8,128)}, f32[256,256]{1,0:T(8,128)}), (f32[256,2048]{1,0:T(8,128)}, f32[256,2048]{1,0:T(8,128)}, f32[256,256]{1,0:T(8,128)})) %all-reduce.11.cloned.1.call-update) | async-done | bytes 4456464 | tf_op jit(solution)/shard_map/psum | solution.py:9
  246.1 1.5 fusion.22
  247.6 2.3 gather_fusion
  250.0 0.6 fusion.37
  250.5 0.6 fusion.35
  251.3 2.3 gather_fusion.1
  253.7 23.6 %convolution_subtract_fusion.1 = f32[1024,2048]{1,0:T(8,128)S(1)} fusion(f32[1024,2048]{1,0:T(8,128)} %param.18, f32[1024,256]{1,0:T(8,128)S(1)} %get-tuple-element.131, f32[256,2048]{1,0:T(8,128)} %get-tuple-element.113, pred[2048]{0:T(1024)(128)(4,1)S(1)} %lt.46), kind=kOutput, calls=%fused_computation.9 | convolution fusion | flops 6445072384 | bytes 19924992 | tf_op jit(solution)/shard_map/dot_general | solution.py:13
  277.4 2.5 fusion.3
  279.9 1.0 fusion.10
  280.9 3.4 copy-done
  284.3 1.1 slice_select_fusion.6
  285.7 50.5 %all-reduce.13.cloned.1.call-done = (f32[1024,256]{1,0:T(8,128)}, f32[1024,256]{1,0:T(8,128)}) async-done(((f32[1024,256]{1,0:T(8,128)}, f32[1024,256]{1,0:T(8,128)}), (f32[1024,256]{1,0:T(8,128)}, f32[1024,256]{1,0:T(8,128)})) %all-reduce.13.cloned.1.call-update) | async-done | bytes 2097168 | tf_op jit(solution)/shard_map/psum | solution.py:9
  336.2 2.6 slice_select_fusion.5
  338.8 3.5 convolution_subtract_fusion.6
  342.3 11.0 %fusion.4 = f32[256,2048]{1,0:T(8,128)} fusion(f32[1024,256]{1,0:T(8,128)S(1)} %get-tuple-element.133, f32[1024,2048]{1,0:T(8,128)} %param.17, f32[1024,2048]{1,0:T(8,128)} %copy-done, pred[]{:T(512)S(6)} %eq.41, pred[2048]{0:T(1024)(128)(4,1)S(1)} %lt.49), kind=kOutput, calls=%fused_computation.17 | convolution fusion | flops 6444023808 | bytes 13633537 | tf_op jit(solution)/shard_map/dot_general | solution.py:13
  353.3 0.9 copy-done.8
  354.2 4.1 while.11
  354.2 0.7 fusion.114
  354.9 1.3 bitcast_dynamic-update-slice_fusion.5
  356.3 0.7 fusion.114
  357.0 1.3 bitcast_dynamic-update-slice_fusion.5
  358.3 19.7 %custom-call.13 = f32[2,128,128]{1,2,0:T(8,128)S(1)} custom-call(f32[2,128,128]{2,1,0:T(8,128)S(1)} %get-tuple-element.93), custom_call_target="InvertDiagBlocksLowerTriangular" | custom-call | tf_op jit(solution)/shard_map/triangular_solve/custom-call.1 | solution.py:45
  378.0 0.7 compare_reduce_fusion
  379.6 137.9 %all-reduce.9.cloned.1.call-done = (f32[256,2048]{1,0:T(8,128)}, f32[256,2048]{1,0:T(8,128)}, f32[256,256]{1,0:T(8,128)}) async-done(((f32[256,2048]{1,0:T(8,128)}, f32[256,2048]{1,0:T(8,128)}, f32[256,256]{1,0:T(8,128)}), (f32[256,2048]{1,0:T(8,128)}, f32[256,2048]{1,0:T(8,128)}, f32[256,256]{1,0:T(8,128)})) %all-reduce.9.cloned.1.call-update) | async-done | bytes 4456464 | tf_op jit(solution)/shard_map/psum | solution.py:9
  517.5 11.8 %convolution_subtract_fusion = f32[1024,2048]{1,0:T(8,128)} fusion(f32[1024,2048]{1,0:T(8,128)} %copy-done, f32[1024,256]{1,0:T(8,128)S(1)} %get-tuple-element.133, f32[256,2048]{1,0:T(8,128)} %get-tuple-element.110, pred[2048]{0:T(1024)(128)(4,1)S(1)} %lt.49), kind=kOutput, calls=%fused_computation.8 | convolution fusion | flops 6445072384 | bytes 19924992 | tf_op jit(solution)/shard_map/dot_general | solution.py:13
  529.3 0.6 fusion.26
  529.9 2.3 gather_fusion.2
  532.3 0.6 fusion.32
  532.8 0.6 fusion.30
  533.5 0.7 copy-done.4
  534.1 0.8 copy.7
  535.0 1.1 bitcast_add_fusion
  536.0 2.3 gather_fusion.3
  538.5 5.5 fusion.1
  544.1 3.1 fusion.11
  (64 shorter events, 3.8 us)
Async XLA Ops:
  6.5 58.2 %all-reduce.15.cloned.1.call-start = ((), (), s32[]{:S(2)}) async-start(), calls=%async_computation.3 | async-start | bytes 4194304 | tf_op jit(solution)/shard_map/psum | solution.py:9
  10.3 235.7 %all-reduce.11.cloned.1.call-start = ((), (), s32[]{:S(2)}) async-start(), calls=%async_computation.1 | async-start | bytes 8912896 | tf_op jit(solution)/shard_map/psum | solution.py:9
  10.6 54.2 %copy-start.1 = (f32[2,256,256]{2,1,0:T(8,128)S(1)}, f32[2,256,256]{2,1,0:T(8,128)}, u32[]{:S(2)}) copy-start(f32[2,256,256]{2,1,0:T(8,128)} %param.19) | copy-start | bytes 1572868
  64.8 2.6 copy-start.9
  81.9 254.2 %all-reduce.13.cloned.1.call-start = ((), (), s32[]{:S(2)}) async-start(), calls=%async_computation.2 | async-start | bytes 4194304 | tf_op jit(solution)/shard_map/psum | solution.py:9
  107.2 138.9 %copy-start.5 = (f32[256,256]{1,0:T(8,128)}, f32[256,256]{1,0:T(8,128)S(1)}, u32[]{:S(2)}) copy-start(f32[256,256]{1,0:T(8,128)S(1)} %fusion.50) | copy-start | bytes 786436
  253.7 23.7 %copy-start.2 = (f32[256,2048]{1,0:T(8,128)S(1)}, f32[256,2048]{1,0:T(8,128)}, u32[]{:S(2)}) copy-start(f32[256,2048]{1,0:T(8,128)} %get-tuple-element.113) | copy-start | bytes 6291460
  253.7 23.7 %copy-start.7 = (f32[256,2048]{1,0:T(8,128)S(1)}, f32[256,2048]{1,0:T(8,128)}, u32[]{:S(2)}) copy-start(f32[256,2048]{1,0:T(8,128)} %get-tuple-element.114) | copy-start | bytes 6291460
  280.9 3.4 copy-start
  285.4 232.1 %all-reduce.9.cloned.1.call-start = ((), (), s32[]{:S(2)}) async-start(), calls=%async_computation | async-start | bytes 8912896 | tf_op jit(solution)/shard_map/psum | solution.py:9
  336.2 2.6 copy-start.10
  353.3 0.9 copy-start.8
  353.3 25.4 %copy-start.6 = (f32[256,256]{1,0:T(8,128)S(1)}, f32[256,256]{1,0:T(8,128)}, u32[]{:S(2)}) copy-start(f32[256,256]{1,0:T(8,128)} %copy-done.5) | copy-start | bytes 786436
  517.5 11.8 %copy-start.11 = (f32[256,256]{1,0:T(8,128)S(1)}, f32[256,256]{1,0:T(8,128)}, u32[]{:S(2)}) copy-start(f32[256,256]{1,0:T(8,128)} %get-tuple-element.112) | copy-start | bytes 786436
  533.4 0.7 copy-start.4
  534.1 4.4 copy-start.3
Sparse Core Ops, SparseCore 0:
  10.5 54.2 all-reduce.14
  82.0 163.9 all-reduce.10
  285.6 50.5 all-reduce.12
  353.4 164.0 all-reduce.8
where the time goes:
time: 553 us; the launch traced here: 554 us
  waiting for transfers between devices  376 us (68%)
  matrix products  83.8 us (15%)
  other arithmetic  56.6 us (10%)
  local copies, waits for them, and re-layouts  23.5 us (4%)
  between operations  13.7 us (2%)
    psum x4, waiting for transfers between devices, broadcast(): return lax.psum(kept, axis)  376 us
    dot_general x16, matrix products, product(): jnp.dot(left, right, precision=lax.Precision.HIGHEST, preferred_element_t...  82.1 us
    another operation x4, other arithmetic, panel_step(): lax.linalg.triangular_solve(inverse_tile, identity, left_side=True, lower...  40.1 us
  transfers between devices with their start and end apart: 4, of which 4 were waited for; matrix products, arithmetic and copies ran while one was open for 10% of the time, Pallas kernels for 0%

commit v1 on v0

v1 whole, which is shorter than its diff:
```python
import jax
import jax.numpy as jnp
from jax import lax
from jax.sharding import PartitionSpec as P


def product(left, right):
    return jnp.dot(left, right, precision=lax.Precision.HIGH, preferred_element_type=jnp.float32)


def product_tn(left, right):
    return lax.dot_general(
        left,
        right,
        (((0,), (0,)), ((), ())),
        precision=lax.Precision.HIGH,
        preferred_element_type=jnp.float32,
    )


def exact(left, right):
    return jnp.dot(left, right, precision=lax.Precision.HIGHEST, preferred_element_type=jnp.float32)


def halved_lower(matrix):
    return jnp.tril(matrix) - 0.5 * jnp.diag(jnp.diagonal(matrix))


def lower_inverse(tile):
    width = tile.shape[0]
    diag = jnp.diagonal(tile)
    identity = jnp.eye(width, dtype=jnp.float32)
    power = jnp.tril(tile, -1) / diag[:, None]
    total = identity - power
    reach = 2
    while reach < width:
        power = exact(power, power)
        total = total + exact(total, power)
        reach *= 2
    return total / diag[None, :]


def symmetric(inverse_tile, factor_diag, diag_total):
    inner = halved_lower(exact(factor_diag.T, jnp.tril(diag_total)))
    wmat = exact(exact(inverse_tile.T, inner), inverse_tile)
    return wmat + wmat.T


def per_device(factor, adjoint, inverse):
    width = inverse.shape[-1]
    row, col = lax.axis_index("row"), lax.axis_index("col")
    last_row, last_col = lax.axis_size("row") - 1, lax.axis_size("col") - 1
    top, side = factor.shape[0] // 2, factor.shape[1] // 2
    inv_one, inv_two = inverse[0], inverse[1]
    d_one, d_two = lower_inverse(inv_one), lower_inverse(inv_two)

    col_one = jnp.where(col == 0, adjoint[top:, side : side + width], 0.0)
    col_two = jnp.where(col == last_col, adjoint[top:, side - width : side], 0.0)
    row_one = jnp.where(row == 0, factor[top : top + width, :side], 0.0)
    row_two = jnp.where(row == last_row, factor[top - width : top, :side], 0.0)
    corner = jnp.where(
        (row == 0) & (col == last_col), factor[top : top + width, side - width : side], 0.0
    )
    cols = lax.psum(jnp.concatenate([col_one, col_two], 1), "col")
    corner = lax.psum(corner, ("row", "col"))
    rows = lax.psum(jnp.concatenate([row_one, row_two], 0), "row")

    is_top = (jnp.arange(top) < width)[:, None] & (row == 0)
    a_one = jnp.where(is_top, 0.0, product(cols[:, :width], inv_one))
    a_two = jnp.where(is_top, 0.0, product(cols[:, width:] - product(a_one, corner), inv_two))
    both = jnp.concatenate([a_one, a_two], 1)
    lower = factor[top:]
    part = product_tn(both, lower[:, : side + width])
    tile_last = slice(side - width, side)
    diag_one = jnp.where(
        col == 0,
        jnp.where(row == 0, adjoint[top : top + width, side : side + width], 0.0)
        - part[:width, side : side + width],
        0.0,
    )
    edge_one = jnp.where(
        col == last_col,
        jnp.where(row == 0, adjoint[top : top + width, tile_last], 0.0) - part[:width, tile_last],
        0.0,
    )
    diag_two = jnp.where(
        col == last_col,
        jnp.where(row == last_row, adjoint[top - width : top, tile_last], 0.0)
        - part[width:, tile_last],
        0.0,
    )
    tiles = lax.psum(jnp.concatenate([diag_one, edge_one, diag_two], 1), ("row", "col"))
    sums = lax.psum(part[:, :side], "row")

    r_one, r_two = rows[:width], rows[width:]
    left = ((jnp.arange(side) < side - width) | (col != last_col))[None, :]
    r_two = jnp.where(left, r_two, 0.0)
    sym_one = symmetric(inv_one, d_one, tiles[:, :width])
    edge = tiles[:, width : 2 * width] - exact(sym_one, corner)
    a_edge = exact(edge, inv_two)
    diag_total = tiles[:, 2 * width :] - exact(a_edge.T, corner)
    sym_two = symmetric(inv_two, d_two, diag_total)

    new_top = sums[:width] + product(sym_one, r_one)
    a_two = jnp.where(is_top, jnp.pad(a_edge, ((0, top - width), (0, 0))), a_two)
    quad = adjoint[top:, :side] - product(
        jnp.concatenate([a_one, a_two], 1), jnp.concatenate([r_one, r_two], 0)
    )
    quad = quad.at[:width].add(jnp.where(row == 0, -new_top, 0.0))
    quad = quad.at[:, tile_last].set(jnp.where(col == last_col, a_two, quad[:, tile_last]))
    new_row = adjoint[top - width : top, :side] - (
        sums[width:]
        + product(
            jnp.concatenate([a_edge.T, sym_two], 1), jnp.concatenate([r_one, r_two], 0)
        )
    )
    new_row = new_row.at[:, tile_last].set(
        jnp.where(col == last_col, halved_lower(sym_two), new_row[:, tile_last])
    )
    new_row = jnp.where(row == last_row, new_row, adjoint[top - width : top, :side])
    new_col = a_one.at[:width].set(jnp.where(row == 0, halved_lower(sym_one), a_one[:width]))
    new_col = jnp.where(col == 0, new_col, adjoint[top:, side : side + width])
    out = adjoint.at[top:, :side].set(quad)
    out = out.at[top - width : top, :side].set(new_row)
    return out.at[top:, side : side + width].set(new_col)


def solution(mesh):
    return jax.shard_map(
        per_device,
        mesh=mesh,
        in_specs=(P("row", "col"), P("row", "col"), P()),
        out_specs=P("row", "col"),
        check_vma=False,
    )
```

time: 553 us -> 514 us (0.929)
  other arithmetic: 56.6 us -> 12.8 us
  matrix products: 83.8 us -> 40.1 us
  local copies, waits for them, and re-layouts: 23.5 us -> 56.9 us
  waiting for transfers between devices: 376 us -> 389 us
    dot_general x16 -> x44, matrix products: 82.1 us -> 40.1 us  [the longest x37 25.2 us: exact(): jnp.dot(left, right, precision=lax.Precision.HIGHEST, preferred_element_t...]
    another operation x6 -> x0, other arithmetic: 41.5 us -> none  [the longest x4 40.1 us: panel_step(): lax.linalg.triangular_solve(inverse_tile, identity, left_side=True, lower...]
    psum x4, waiting for transfers between devices: 376 us -> 389 us  [the longest x1 142 us: per_device(): rows = lax.psum(jnp.concatenate([row_one, row_two], 0), 'row')]
    unnamed x24 -> x67, local copies, waits for them, and re-layouts: 5.02 us -> 18.2 us
    slice x0 -> x8, local copies, waits for them, and re-layouts: none -> 11.9 us  [the longest x1 2.75 us: per_device(): row_one = jnp.where(row == 0, factor[top:top + width, :side], 0.0)]
    another operation x15 -> x0, local copies, waits for them, and re-layouts: 7.79 us -> none  [panel_step(): lax.linalg.triangular_solve(inverse_tile, identity, left_side=True, lower...]
    scatter x0 -> x4, local copies, waits for them, and re-layouts: none -> 6.97 us  [the longest x1 3.25 us: per_device(): out = adjoint.at[top:, :side].set(quad)]
  transfers between devices with their start and end apart: 4 -> 4, of which waited for: 4 -> 4; matrix products, arithmetic and copies ran while one was open for 10% -> 13% of each run, Pallas kernels for 0% -> 0%
where the time goes in v1:
time: 514 us; the launch traced here: 513 us
  waiting for transfers between devices  389 us (76%)
  local copies, waits for them, and re-layouts  56.9 us (11%)
  matrix products  40.1 us (8%)
  between operations  14 us (3%)
  other arithmetic  12.8 us (2%)
    psum x1, waiting for transfers between devices, per_device(): rows = lax.psum(jnp.concatenate([row_one, row_two], 0), 'row')  142 us
    psum x1, waiting for transfers between devices, per_device(): corner = lax.psum(corner, ('row', 'col'))  130 us
    psum x1, waiting for transfers between devices, per_device(): lax.psum(jnp.concatenate([diag_one, edge_one, diag_two], 1), ('row', 'col'))  110 us
    dot_general x37, matrix products, exact(): jnp.dot(left, right, precision=lax.Precision.HIGHEST, preferred_element_t...  25.2 us
    unnamed x67, local copies, waits for them, and re-layouts  18.2 us
    dot_general x6, matrix products, product(): jnp.dot(left, right, precision=lax.Precision.HIGH, preferred_element_type...  10.4 us
  transfers between devices with their start and end apart: 4, of which 4 were waited for; matrix products, arithmetic and copies ran while one was open for 13% of the time, Pallas kernels for 0%

profile of v1, /device:TPU:0, one launch (start us, length us, event | category | flops | bytes accessed | tf_op | source)
XLA Modules:
  0.0 513.1 jit_solution(8892346213669857781)
XLA Ops:
  6.5 7.9 %copy.123 = f32[1024,2048]{1,0:T(8,128)} copy(f32[1024,2048]{1,0:T(8,128)} %param.18) | data formatting | bytes 16777216
  14.4 1.3 fusion.103
  16.2 1.0 pad_maximum_fusion.14
  17.4 1.0 slice.237
  19.3 1.2 fusion.102
  20.7 2.4 gather_fusion
  23.7 1.3 convolution_add_fusion.14
  25.4 2.8 fusion.104
  28.3 2.5 gather_fusion.2
  31.5 1.3 convolution_add_fusion.7
  39.7 1.1 fusion.112
  40.7 1.3 convolution_add_fusion.9
  42.4 1.6 copy.108
  46.3 1.3 convolution_add_fusion.4
  47.6 1.5 broadcast_select_fusion
  49.1 7.1 %all-reduce.7.cloned.1.call-done = f32[512,512]{0,1:T(8,128)} async-done(((f32[512,512]{0,1:T(8,128)}), f32[512,512]{0,1:T(8,128)}) %all-reduce.7.cloned.1.call-update) | async-done | bytes 1048592 | tf_op jit(solution)/shard_map/psum | solution.py:64
  56.2 1.5 convolution_select_fusion.1
  57.7 130.3 %all-reduce.9.cloned.1.call-done = f32[256,256]{0,1:T(8,128)} async-done(((f32[256,256]{0,1:T(8,128)}), f32[256,256]{0,1:T(8,128)}) %all-reduce.9.cloned.1.call-update) | async-done | bytes 262160 | tf_op jit(solution)/shard_map/psum | solution.py:65
  188.0 1.5 convolution_subtract_fusion
  190.1 4.5 fusion
  194.8 0.9 pad_maximum_fusion.15
  195.8 3.2 pad_maximum_fusion
  199.0 1.1 fusion.117
  200.1 1.6 slice.282
  201.7 1.7 slice.230
  203.4 2.4 slice.255
  205.8 1.9 copy.98
  207.6 2.6 copy.109
  212.5 1.3 fusion.12
  213.8 110.1 %all-reduce.11.cloned.1.call-done = f32[256,768]{0,1:T(8,128)} async-done(((f32[256,768]{0,1:T(8,128)}), f32[256,768]{0,1:T(8,128)}) %all-reduce.11.cloned.1.call-update) | async-done | bytes 786448 | tf_op jit(solution)/shard_map/psum | solution.py:92
  323.9 1.4 fusion.23
  325.4 2.3 gather_fusion.1
  329.0 2.4 gather_fusion.5
  332.9 1.4 fusion.119
  334.5 2.3 gather_fusion.3
  338.0 2.6 gather_fusion.4
  341.5 141.7 %all-reduce.13.cloned.1.call-done = (f32[512,1024]{0,1:T(8,128)}, f32[512,1024]{0,1:T(8,128)}) async-done(((f32[512,1024]{0,1:T(8,128)}, f32[512,1024]{0,1:T(8,128)}), (f32[512,1024]{0,1:T(8,128)}, f32[512,1024]{0,1:T(8,128)})) %all-reduce.13.cloned.1.call-update) | async-done | bytes 4194320 | tf_op jit(solution)/shard_map/psum | solution.py:66
  483.2 1.9 fusion.105
  485.5 1.9 fusion.4
  487.5 0.9 broadcast_select_fusion.5
  488.4 2.0 copy.81
  490.5 2.7 fusion.10
  493.2 2.3 fusion.6
  495.6 1.1 broadcast_select_fusion.2
  496.7 2.6 copy.80
  499.4 1.9 copy.69
  501.3 3.2 constant_dynamic-update-slice_fusion.1
  504.5 1.0 constant_dynamic-update-slice_fusion
  (120 shorter events, 22.3 us)
Async XLA Ops:
  6.5 49.7 %all-reduce.7.cloned.1.call-start = ((), (), s32[]{:S(2)}) async-start(), calls=%async_computation | async-start | bytes 2097152 | tf_op jit(solution)/shard_map/psum | solution.py:64
  15.9 1.4 copy-start.12
  17.3 3.3 copy-start
  17.3 170.7 %all-reduce.9.cloned.1.call-start = ((), (), s32[]{:S(2)}) async-start(), calls=%async_computation.1 | async-start | bytes 524288 | tf_op jit(solution)/shard_map/psum | solution.py:65
  19.3 304.6 %all-reduce.11.cloned.1.call-start = ((), (), s32[]{:S(2)}) async-start(), calls=%async_computation.2 | async-start | bytes 1572864 | tf_op jit(solution)/shard_map/psum | solution.py:92
  31.4 4.6 copy-start.26
  42.0 2.3 copy-start.25
  190.0 4.6 copy-start.10
  190.0 4.6 copy-start.19
  190.0 4.6 copy-start.20
  190.1 4.6 copy-start.21
  195.7 287.4 %all-reduce.13.cloned.1.call-start = ((), (), s32[]{:S(2)}) async-start(), calls=%async_computation.3 | async-start | bytes 8388608 | tf_op jit(solution)/shard_map/psum | solution.py:66
  207.6 2.6 copy-start.18
  207.6 3.2 copy-start.14
  207.6 4.3 copy-start.23
  207.6 4.3 copy-start.24
  211.9 115.9 %copy-start.1 = (f32[2,256,256]{2,1,0:T(8,128)S(1)}, f32[2,256,256]{2,1,0:T(8,128)}, u32[]{:S(2)}) copy-start(f32[2,256,256]{2,1,0:T(8,128)} %param.19) | copy-start | bytes 1572868
  327.8 3.6 copy-start.16
  327.8 3.6 copy-start.22
  336.8 3.8 copy-start.11
  483.2 2.2 copy-start.7
  483.2 2.3 copy-start.8
  485.1 2.3 copy-start.2
  485.1 2.3 copy-start.4
  485.5 2.1 copy-start.13
  490.4 2.7 copy-start.3
  490.4 2.7 copy-start.5
  490.5 2.7 copy-start.6
  495.6 3.7 copy-start.9
  501.3 3.3 copy-start.15
  504.5 1.2 copy-start.17
Sparse Core Ops, SparseCore 0:
  17.4 38.7 all-reduce.6
  62.6 125.3 all-reduce.8
  195.9 128.0 all-reduce.10
  327.5 155.6 all-reduce.12

commit v2 on v0

v2 whole, which is shorter than its diff:
```python
import functools

import jax
import jax.numpy as jnp
from jax import lax
from jax.experimental import pallas as pl
from jax.experimental.pallas import tpu as pltpu
from jax.sharding import PartitionSpec as P

F32 = jnp.float32
MESH = pl.DeviceIdType.MESH
SLOTS = 10
COL_CHUNKS = 4
CORNER_CHUNKS = 4
ROW_CHUNKS = 8
CRIT_CHUNKS = 2


def split(value):
    high = value.astype(jnp.bfloat16)
    return high, (value - high.astype(F32)).astype(jnp.bfloat16)


def product(left, right):
    left_high, left_low = split(left)
    right_high, right_low = split(right)
    dot = functools.partial(jnp.dot, preferred_element_type=F32)
    return dot(left_high, right_high) + (dot(left_high, right_low) + dot(left_low, right_high))


def exact(left, right):
    return jnp.dot(left, right, precision=lax.Precision.HIGHEST, preferred_element_type=F32)


def iotas(width):
    rows = lax.broadcasted_iota(jnp.int32, (width, width), 0)
    cols = lax.broadcasted_iota(jnp.int32, (width, width), 1)
    return rows, cols


def halved_lower(matrix):
    rows, cols = iotas(matrix.shape[0])
    return jnp.where(rows > cols, matrix, jnp.where(rows == cols, 0.5 * matrix, 0.0))


def lower_inverse(tile):
    width = tile.shape[0]
    rows, cols = iotas(width)
    diagonal = jnp.where(rows == cols, tile, 0.0)
    power = jnp.where(rows > cols, tile, 0.0) / jnp.sum(diagonal, axis=1, keepdims=True)
    total = jnp.where(rows == cols, 1.0, 0.0) - power
    reach = 2
    while reach < width:
        power = exact(power, power)
        total = total + exact(total, power)
        reach *= 2
    return total / jnp.sum(diagonal, axis=0, keepdims=True)


def symmetric(inverse_tile, factor_diag, diag_total):
    rows, cols = iotas(inverse_tile.shape[0])
    inner = halved_lower(exact(factor_diag.T, jnp.where(rows >= cols, diag_total, 0.0)))
    wmat = exact(exact(inverse_tile.T, inner), inverse_tile)
    return wmat + wmat.T


class Line:
    def __init__(self, axis):
        self.axis = axis
        self.count = lax.axis_size(axis)
        self.place = lax.axis_index(axis)
        self.mine = lax.rem(self.place, 2)
        step = 2 - 4 * self.mine
        self.partner = self.place + 1 - 2 * self.mine
        self.prev = self.place - step
        self.next = self.place + step
        self.first = self.place == self.mine * (self.count - 1)
        self.last = self.place == (self.count - 2) * (1 - self.mine) + self.mine


def row_kernel(
    factor, adjoint, inverse, a_out, r_out, fix_out, phi_out,
    lower, cols, offdiag, rows_buf, corner, part, from_partner, from_next, crit, ldiag,
    edge_in, edge_own, dmat, local_sem, load_sem,
    cols_recv, cols_send, corner_crecv, corner_csend, corner_rrecv, corner_rsend,
    rows_recv, rows_send, leaf_send, chain_send, partner_recv, next_recv,
    crit_recv, crit_send, edge_sems, out_sem,
):
    width = inverse.shape[-1]
    half = width // 2
    top, side = cols.shape[1], rows_buf.shape[2]
    row, col = Line("row"), Line("col")
    top_row, bottom_row = row.place == 0, row.place == row.count - 1
    end_row = top_row | bottom_row

    def remote(src, dst, send, recv, line, target):
        return pltpu.make_async_remote_copy(
            src_ref=src, dst_ref=dst, send_sem=send, recv_sem=recv,
            device_id={line.axis: target}, device_id_type=MESH,
        )

    barrier = pltpu.get_barrier_semaphore()
    for line in (row, col):
        pl.semaphore_signal(barrier, inc=1, device_id={line.axis: line.partner}, device_id_type=MESH)

        @pl.when(jnp.logical_not(line.first))
        def _():
            pl.semaphore_signal(barrier, inc=1, device_id={line.axis: line.prev}, device_id_type=MESH)

        @pl.when(jnp.logical_not(line.last))
        def _():
            pl.semaphore_signal(barrier, inc=1, device_id={line.axis: line.next}, device_id_type=MESH)

    @pl.when(end_row)
    def _():
        pl.semaphore_signal(
            barrier, inc=1, device_id={"row": row.count - 1 - row.place}, device_id_type=MESH
        )

    lower_load = pltpu.make_async_copy(
        factor.at[pl.ds(top, top), pl.ds(0, side + width)], lower, load_sem
    )
    lower_load.start()
    panel_start = side - width * col.mine
    row_start = top - width * row.mine

    @pl.when(col.first)
    def _():
        copy = pltpu.make_async_copy(
            adjoint.at[pl.ds(top, top), pl.ds(pl.multiple_of(panel_start, width), width)],
            cols.at[col.mine], local_sem.at[0],
        )
        copy.start()
        copy.wait()

    @pl.when(top_row & (col.place == col.count - 1))
    def _():
        copy = pltpu.make_async_copy(
            factor.at[pl.ds(top, width), pl.ds(side - width, width)], corner, local_sem.at[1]
        )
        copy.start()
        copy.wait()

    @pl.when(row.first)
    def _():
        copy = pltpu.make_async_copy(
            factor.at[pl.ds(pl.multiple_of(row_start, width), width), pl.ds(0, side)],
            rows_buf.at[row.mine], local_sem.at[2],
        )
        copy.start()
        copy.wait()

    @pl.when(bottom_row)
    def _():
        copy = pltpu.make_async_copy(
            adjoint.at[pl.ds(top - width, width), pl.ds(side - width, width)], ldiag, local_sem.at[3]
        )
        copy.start()
        copy.wait()

    expected = 2 + sum(
        jnp.where(line.first, 0, 1) + jnp.where(line.last, 0, 1) for line in (row, col)
    )
    pl.semaphore_wait(barrier, expected + jnp.where(end_row, 1, 0))

    def pass_on(line, buf, size, chunk, recv, send, panel=None):
        lead = line.mine if panel is None else panel
        ref = buf.at[lead, pl.ds(pl.multiple_of(chunk * size, 8), size)]

        @pl.when(jnp.logical_not(line.first))
        def _():
            remote(ref, ref, send.at[0, chunk], recv.at[lead, chunk], line, line.partner).wait_recv()

        @pl.when(jnp.logical_not(line.last))
        def _():
            remote(ref, ref, send.at[0, chunk], recv.at[lead, chunk], line, line.next).start()

        remote(ref, ref, send.at[1, chunk], recv.at[lead, chunk], line, line.partner).start()

    def take(line, buf, size, chunk, recv, send):
        lead = 1 - line.mine
        ref = buf.at[lead, pl.ds(pl.multiple_of(chunk * size, 8), size)]
        remote(ref, ref, send.at[1, chunk], recv.at[lead, chunk], line, line.partner).wait_recv()

    def finish_sends(line, buf, size, chunks, send, recv):
        def body(chunk, carry):
            ref = buf.at[line.mine, pl.ds(pl.multiple_of(chunk * size, 8), size)]

            @pl.when(jnp.logical_not(line.last))
            def _():
                remote(ref, ref, send.at[0, chunk], recv.at[0, chunk], line, line.next).wait_send()

            remote(ref, ref, send.at[1, chunk], recv.at[0, chunk], line, line.partner).wait_send()
            return carry

        lax.fori_loop(0, chunks, body, 0)

    def loop(start, stop, step):
        def body(index, carry):
            step(index)
            return carry

        lax.fori_loop(start, stop, body, 0)

    cols_size = top // COL_CHUNKS
    rows_size = width // ROW_CHUNKS
    corner_size = width // CORNER_CHUNKS
    loop(0, COL_CHUNKS, lambda c: pass_on(col, cols, cols_size, c, cols_recv, cols_send))

    def corner_ref(chunk):
        return corner.at[pl.ds(pl.multiple_of(chunk * corner_size, 8), corner_size)]

    def corner_cols(chunk):
        ref = corner_ref(chunk)

        @pl.when(col.mine == 1)
        def _():
            @pl.when(jnp.logical_not(col.first))
            def _():
                remote(
                    ref, ref, corner_csend.at[0, chunk], corner_crecv.at[chunk], col, col.partner
                ).wait_recv()

            @pl.when(jnp.logical_not(col.last))
            def _():
                remote(
                    ref, ref, corner_csend.at[0, chunk], corner_crecv.at[chunk], col, col.next
                ).start()

            remote(
                ref, ref, corner_csend.at[1, chunk], corner_crecv.at[chunk], col, col.partner
            ).start()

        @pl.when(col.mine == 0)
        def _():
            remote(
                ref, ref, corner_csend.at[1, chunk], corner_crecv.at[chunk], col, col.partner
            ).wait_recv()

    def corner_rows(chunk):
        ref = corner_ref(chunk)

        @pl.when(jnp.logical_not(top_row))
        def _():
            remote(
                ref, ref, corner_rsend.at[0, chunk], corner_rrecv.at[chunk], row, row.partner
            ).wait_recv()

        @pl.when(row.mine == 0)
        def _():
            @pl.when(jnp.logical_not(row.last))
            def _():
                remote(
                    ref, ref, corner_rsend.at[0, chunk], corner_rrecv.at[chunk], row, row.next
                ).start()

            remote(
                ref, ref, corner_rsend.at[1, chunk], corner_rrecv.at[chunk], row, row.partner
            ).start()

    def corner_step(chunk):
        @pl.when(top_row)
        def _():
            corner_cols(chunk)

        corner_rows(chunk)

    @pl.when(top_row)
    def _():
        loop(0, CORNER_CHUNKS, corner_step)

    @pl.when(row.first)
    def _():
        loop(0, ROW_CHUNKS, lambda c: pass_on(row, rows_buf, rows_size, c, rows_recv, rows_send))

    loop(0, COL_CHUNKS, lambda c: take(col, cols, cols_size, c, cols_recv, cols_send))
    lower_load.wait()

    def own_terms(panel, first_slot):
        left = offdiag[panel].T
        left_high, left_low = split(left)
        dot = functools.partial(jnp.dot, preferred_element_type=F32)

        def body(tile, carry):
            start = jnp.where(tile == 0, side, jnp.where(tile == 1, side - width, (tile - 2) * width))
            right = lower[:, pl.ds(pl.multiple_of(start, width), width)]
            high, low = split(right)
            value = dot(left_high, high) + (dot(left_high, low) + dot(left_low, high))
            part[panel, 2 * tile] = value[:half]
            part[panel, 2 * tile + 1] = value[half:]
            return carry

        lax.fori_loop(first_slot // 2, SLOTS // 2, body, 0)

        @pl.when(row.mine == 1 - panel)
        def _():
            send_start = jnp.where((col.place == 0) & (panel == 0), 0, 2)
            loop(
                send_start, SLOTS,
                lambda s: remote(
                    part.at[panel, s], from_partner.at[s], leaf_send.at[s], partner_recv.at[s],
                    row, row.partner,
                ).start(),
            )

    offdiag[0] = product(cols[0], inverse[0])

    @pl.when(top_row)
    def _():
        offdiag[0, :width] = jnp.zeros((width, width), F32)

    own_terms(0, 0)

    @pl.when(jnp.logical_not(top_row))
    def _():
        loop(0, CORNER_CHUNKS, corner_step)

    offdiag[1] = product(cols[1] - product(offdiag[0], corner[...]), inverse[1])

    @pl.when(top_row)
    def _():
        offdiag[1, :width] = jnp.zeros((width, width), F32)

    own_terms(1, 2)

    @pl.when(end_row)
    def _():
        dmat[...] = lower_inverse(inverse[row.mine])

    slot_start = jnp.where((col.place == 0) & (row.mine == 0), 0, 2)

    def reduce_step(slot):
        mine = part.at[row.mine, slot]
        remote(
            mine, from_partner.at[slot], leaf_send.at[slot], partner_recv.at[slot], row, row.partner
        ).wait_recv()
        part[row.mine, slot] = part[row.mine, slot] + from_partner[slot]

        @pl.when(jnp.logical_not(row.last))
        def _():
            remote(
                mine, from_next.at[slot], chain_send.at[slot], next_recv.at[slot], row, row.partner
            ).wait_recv()
            part[row.mine, slot] = part[row.mine, slot] + from_next[slot]

        @pl.when(jnp.logical_not(row.first))
        def _():
            remote(
                mine, from_next.at[slot], chain_send.at[slot], next_recv.at[slot], row, row.prev
            ).start()

    def stream_step(index):
        @pl.when((index < ROW_CHUNKS) & jnp.logical_not(row.first))
        def _():
            pass_on(row, rows_buf, rows_size, index, rows_recv, rows_send)

        @pl.when(index >= slot_start)
        def _():
            reduce_step(index)

    loop(0, 4, stream_step)
    crit_size = width // CRIT_CHUNKS

    @pl.when(end_row)
    def _():
        @pl.when(col.first)
        def _():
            lead = col.mine
            slot = 2 * jnp.maximum(lead, row.mine)
            for piece in range(2):
                span = slice(half * piece, half * (piece + 1))
                value = part[row.mine, slot + piece]
                crit[lead, span] = jnp.where(bottom_row, ldiag[span] - value, value)

        loop(0, CRIT_CHUNKS, lambda c: pass_on(col, crit, crit_size, c, crit_recv, crit_send))
        loop(0, CRIT_CHUNKS, lambda c: take(col, crit, crit_size, c, crit_recv, crit_send))

    def edge_copy():
        return remote(
            edge_own, edge_in, edge_sems.at[0], edge_sems.at[1], row, row.count - 1
        )

    @pl.when(top_row)
    def _():
        sym = symmetric(inverse[0], dmat[...], cols[0, :width] - crit[0])
        edge_own[...] = product(cols[1, :width] - crit[1] - product(sym, corner[...]), inverse[1])
        edge_copy().start()
        offdiag[1, :width] = edge_own[...]
        dmat[...] = sym

    loop(4, SLOTS, stream_step)
    loop(0, ROW_CHUNKS, lambda c: take(row, rows_buf, rows_size, c, rows_recv, rows_send))

    outs = [
        pltpu.make_async_copy(offdiag, a_out, out_sem.at[0]),
        pltpu.make_async_copy(rows_buf, r_out, out_sem.at[1]),
    ]
    for copy in outs:
        copy.start()

    @pl.when(bottom_row)
    def _():
        edge_copy().wait_recv()
        edge_t = edge_in[...].T
        edge_own[...] = edge_t
        diag_total = crit[1] - product(edge_t, corner[...])
        dmat[...] = symmetric(inverse[1], dmat[...], diag_total)

    @pl.when(end_row)
    def _():
        phi_out[...] = halved_lower(dmat[...])

        def body(tile, carry):
            slot = jnp.where(tile == side // width - 1, 2, 2 * tile + 4)
            start = pl.multiple_of(tile * width, width)
            value = product(dmat[...], rows_buf[row.mine, :, pl.ds(start, width)])
            fix_out[:half, pl.ds(start, width)] = value[:half] + part[row.mine, slot]
            fix_out[half:, pl.ds(start, width)] = value[half:] + part[row.mine, slot + 1]

            @pl.when(bottom_row)
            def _():
                fix_out[:, pl.ds(start, width)] = fix_out[:, pl.ds(start, width)] + product(
                    edge_own[...], rows_buf[0, :, pl.ds(start, width)]
                )

            return carry

        lax.fori_loop(0, side // width, body, 0)

    finish_sends(col, cols, cols_size, COL_CHUNKS, cols_send, cols_recv)
    finish_sends(row, rows_buf, rows_size, ROW_CHUNKS, rows_send, rows_recv)

    @pl.when(end_row)
    def _():
        finish_sends(col, crit, crit_size, CRIT_CHUNKS, crit_send, crit_recv)

    def corner_finish(chunk):
        ref = corner_ref(chunk)

        @pl.when(top_row & (col.mine == 1))
        def _():
            @pl.when(jnp.logical_not(col.last))
            def _():
                remote(
                    ref, ref, corner_csend.at[0, chunk], corner_crecv.at[chunk], col, col.next
                ).wait_send()

            remote(
                ref, ref, corner_csend.at[1, chunk], corner_crecv.at[chunk], col, col.partner
            ).wait_send()

        @pl.when(row.mine == 0)
        def _():
            @pl.when(jnp.logical_not(row.last))
            def _():
                remote(
                    ref, ref, corner_rsend.at[0, chunk], corner_rrecv.at[chunk], row, row.next
                ).wait_send()

            remote(
                ref, ref, corner_rsend.at[1, chunk], corner_rrecv.at[chunk], row, row.partner
            ).wait_send()

    loop(0, CORNER_CHUNKS, corner_finish)
    leaf_start = jnp.where((col.place == 0) & (row.mine == 1), 0, 2)
    loop(
        leaf_start, SLOTS,
        lambda s: remote(
            part.at[1 - row.mine, s], from_partner.at[s], leaf_send.at[s], partner_recv.at[s],
            row, row.partner,
        ).wait_send(),
    )

    @pl.when(jnp.logical_not(row.first))
    def _():
        loop(
            slot_start, SLOTS,
            lambda s: remote(
                part.at[row.mine, s], from_next.at[s], chain_send.at[s], next_recv.at[s],
                row, row.prev,
            ).wait_send(),
        )

    @pl.when(top_row)
    def _():
        edge_copy().wait_send()

    for copy in outs:
        copy.wait()


def update_kernel(adjoint, offdiag, rows, fix, phi, out):
    step = pl.program_id(0)
    middle = pl.num_programs(0) // 2
    width, side = phi.shape[0], fix.shape[1]
    top_row = lax.axis_index("row") == 0
    bottom_row = lax.axis_index("row") == lax.axis_size("row") - 1
    first_col = lax.axis_index("col") == 0
    last_col = lax.axis_index("col") == lax.axis_size("col") - 1
    out[...] = adjoint[...]

    @pl.when(step >= middle)
    def _():
        pairs = [split(offdiag[panel]) for panel in range(2)]
        dot = functools.partial(jnp.dot, preferred_element_type=F32)

        for start in range(0, side, width):
            value = adjoint[:, start : start + width]
            for panel, (left_high, left_low) in enumerate(pairs):
                high, low = split(rows[panel, :, start : start + width])
                value -= dot(left_high, high) + (dot(left_high, low) + dot(left_low, high))
            out[:, start : start + width] = value

        @pl.when(top_row & (step == middle))
        def _():
            out[:, :side] = out[:, :side] - fix[...]

        @pl.when(last_col)
        def _():
            out[:, side - width : side] = offdiag[1]

        @pl.when(first_col)
        def _():
            out[:, side : side + width] = offdiag[0]

            @pl.when(top_row & (step == middle))
            def _():
                out[:, side : side + width] = phi[...]

    @pl.when(bottom_row & (step == middle - 1))
    def _():
        out[:, :side] = adjoint[:, :side] - fix[...]

        @pl.when(last_col)
        def _():
            out[:, side - width : side] = phi[...]


def per_device(factor, adjoint, inverse):
    width = inverse.shape[-1]
    height, total = factor.shape
    top, side = height // 2, total // 2
    half = width // 2
    any_spec = pl.BlockSpec(memory_space=pl.ANY)
    vmem_spec = pl.BlockSpec(memory_space=pltpu.VMEM)
    dma = pltpu.SemaphoreType.DMA
    offdiag, rows, fix, phi = pl.pallas_call(
        row_kernel,
        out_shape=[
            jax.ShapeDtypeStruct((2, top, width), F32),
            jax.ShapeDtypeStruct((2, width, side), F32),
            jax.ShapeDtypeStruct((width, side), F32),
            jax.ShapeDtypeStruct((width, width), F32),
        ],
        in_specs=[any_spec, any_spec, vmem_spec],
        out_specs=[any_spec, any_spec, vmem_spec, vmem_spec],
        scratch_shapes=[
            pltpu.VMEM((top, side + width), F32),
            pltpu.VMEM((2, top, width), F32),
            pltpu.VMEM((2, top, width), F32),
            pltpu.VMEM((2, width, side), F32),
            pltpu.VMEM((width, width), F32),
            pltpu.VMEM((2, SLOTS, half, width), F32),
            pltpu.VMEM((SLOTS, half, width), F32),
            pltpu.VMEM((SLOTS, half, width), F32),
            pltpu.VMEM((2, width, width), F32),
            pltpu.VMEM((width, width), F32),
            pltpu.VMEM((width, width), F32),
            pltpu.VMEM((width, width), F32),
            pltpu.VMEM((width, width), F32),
            dma((4,)),
            dma,
            dma((2, COL_CHUNKS)),
            dma((2, COL_CHUNKS)),
            dma((CORNER_CHUNKS,)),
            dma((2, CORNER_CHUNKS)),
            dma((CORNER_CHUNKS,)),
            dma((2, CORNER_CHUNKS)),
            dma((2, ROW_CHUNKS)),
            dma((2, ROW_CHUNKS)),
            dma((SLOTS,)),
            dma((SLOTS,)),
            dma((SLOTS,)),
            dma((SLOTS,)),
            dma((2, CRIT_CHUNKS)),
            dma((2, CRIT_CHUNKS)),
            dma((2,)),
            dma((2,)),
        ],
        compiler_params=pltpu.CompilerParams(
            collective_id=0, has_side_effects=True, vmem_limit_bytes=40 * 2**20
        ),
        name="panels",
    )(factor, adjoint, inverse)
    steps = height // width
    middle = steps // 2
    return pl.pallas_call(
        update_kernel,
        grid=(steps,),
        out_shape=jax.ShapeDtypeStruct(adjoint.shape, F32),
        in_specs=[
            pl.BlockSpec((width, total), lambda t: (t, 0)),
            pl.BlockSpec((2, width, width), lambda t: (0, jnp.maximum(t - middle, 0), 0)),
            pl.BlockSpec((2, width, side), lambda t: (0, 0, 0)),
            pl.BlockSpec((width, side), lambda t: (0, 0)),
            pl.BlockSpec((width, width), lambda t: (0, 0)),
        ],
        out_specs=pl.BlockSpec((width, total), lambda t: (t, 0)),
        compiler_params=pltpu.CompilerParams(vmem_limit_bytes=40 * 2**20),
        name="update",
    )(adjoint, offdiag, rows, fix, phi)


def solution(mesh):
    return jax.shard_map(
        per_device,
        mesh=mesh,
        in_specs=(P("row", "col"), P("row", "col"), P()),
        out_specs=P("row", "col"),
        check_vma=False,
    )
```

time: 553 us -> 178 us (0.32)
  waiting for transfers between devices: 376 us -> 0 us
  Pallas kernels: 0 us -> 173 us
  matrix products: 83.8 us -> 0 us
  other arithmetic: 56.6 us -> 0 us
  local copies, waits for them, and re-layouts: 23.5 us -> 4.83 us
  between operations: 13.7 us -> 0.02 us
    psum x4 -> x0, waiting for transfers between devices: 376 us -> none  [broadcast(): return lax.psum(kept, axis)]
    pallas_call x0 -> x2, Pallas kernels: none -> 173 us  [the longest x1 168 us: per_device(): pl.pallas_call(row_kernel, out_shape=[jax.ShapeDtypeStruct((2, top, width...]
    dot_general x16 -> x0, matrix products: 82.1 us -> none  [product(): jnp.dot(left, right, precision=lax.Precision.HIGHEST, preferred_element_t...]
    another operation x6 -> x0, other arithmetic: 41.5 us -> none  [the longest x4 40.1 us: panel_step(): lax.linalg.triangular_solve(inverse_tile, identity, left_side=True, lower...]
    select_n x3 -> x0, other arithmetic: 9.75 us -> none  [broadcast(): jnp.where(lax.axis_index(axis) == source, value, 0).astype(value.dtype)]
    gather x4 -> x0, local copies, waits for them, and re-layouts: 9.37 us -> none  [halved_lower(): return jnp.tril(matrix) - 0.5 * jnp.diag(jnp.diagonal(matrix))]
    another operation x15 -> x0, local copies, waits for them, and re-layouts: 7.79 us -> none  [panel_step(): lax.linalg.triangular_solve(inverse_tile, identity, left_side=True, lower...]
  transfers between devices with their start and end apart: 4 -> 0, of which waited for: 4 -> 0; matrix products, arithmetic and copies ran while one was open for 10% -> 0% of each run, Pallas kernels for 0% -> 0%
where the time goes in v2:
time: 178 us
  Pallas kernels  173 us (97%)
  local copies, waits for them, and re-layouts  4.83 us (3%)
    pallas_call x1, Pallas kernels, per_device(): pl.pallas_call(row_kernel, out_shape=[jax.ShapeDtypeStruct((2, top, width...  168 us
    pallas_call x1, Pallas kernels, per_device(): pl.pallas_call(update_kernel, grid=(steps,), out_shape=jax.ShapeDtypeStru...  5.39 us
    unnamed x6, local copies, waits for them, and re-layouts  4.83 us

profile of v2, /device:TPU:0, one launch (start us, length us, event | category | flops | bytes accessed | tf_op | source)
XLA Modules:
  0.0 177.9 jit_solution(11003471666748559533)
XLA Ops:
  0.0 0.0 copy-start
  0.0 0.0 copy-start.1
  0.0 3.5 %copy-done.1 = f32[1024,2048]{1,0:T(8,128)S(1)} copy-done((f32[1024,2048]{1,0:T(8,128)S(1)}, f32[1024,2048]{1,0:T(8,128)}, u32[]{:S(2)}) %copy-start.1) | copy-done | bytes 8388632
  3.5 0.0 copy-start.2
  3.5 1.3 copy-done.2
  4.8 167.7 %panels.1 = (f32[2,512,256]{2,1,0:T(8,128)S(1)}, f32[2,256,1024]{2,1,0:T(8,128)S(1)}, f32[256,1024]{1,0:T(8,128)S(1)}, f32[256,256]{1,0:T(8,128)S(1)}) custom-call(f32[1024,2048]{1,0:T(8,128)S(1)} %copy-done.1, f32[1024,2048]{1,0:T(8,128)} %adjoint.3, f32[2,256,256]{2,1,0:T(8,128)S(1)} %copy-done.2), custom_call_target="tpu_custom_call" | custom-call | tf_op jit(solution)/shard_map/panels/pallas_call | solution.py:547
  172.5 0.0 copy-done
  172.5 5.4 %update.1 = f32[1024,2048]{1,0:T(8,128)} custom-call(f32[1024,2048]{1,0:T(8,128)S(1)} %copy-done, f32[2,512,256]{2,1,0:T(8,128)S(1)} %get-tuple-element.9.offdiag, f32[2,256,1024]{2,1,0:T(8,128)S(1)} %get-tuple-element.10.rows, f32[256,1024]{1,0:T(8,128)S(1)} %get-tuple-element.11.fix, f32[256,256]{1,0:T(8,128)S(1)} %get-tuple-element.12.phi), custom_call_target="tpu_custom_call" | custom-call | tf_op jit(solution)/shard_map/update/pallas_call | solution.py:597
Async XLA Ops:
  0.0 172.5 %copy-start = (f32[1024,2048]{1,0:T(8,128)S(1)}, f32[1024,2048]{1,0:T(8,128)}, u32[]{:S(2)}) copy-start(f32[1024,2048]{1,0:T(8,128)} %adjoint.3) | copy-start | bytes 25165828
  0.0 3.5 %copy-start.1 = (f32[1024,2048]{1,0:T(8,128)S(1)}, f32[1024,2048]{1,0:T(8,128)}, u32[]{:S(2)}) copy-start(f32[1024,2048]{1,0:T(8,128)} %factor.1) | copy-start | bytes 25165828
  3.5 1.3 copy-start.2

commit v3 on v2

--- a/solution.py
+++ b/solution.py
@@ -276,9 +276,14 @@
     loop(0, COL_CHUNKS, lambda c: take(col, cols, cols_size, c, cols_recv, cols_send))
     lower_load.wait()
 
-    def own_terms(panel, first_slot):
-        left = offdiag[panel].T
-        left_high, left_low = split(left)
+    def leaf_copy(panel, slot):
+        return remote(
+            part.at[panel, slot], from_partner.at[slot], leaf_send.at[slot], partner_recv.at[slot],
+            row, row.partner,
+        )
+
+    def own_terms(panel, first_tile, between):
+        left_high, left_low = split(offdiag[panel].T)
         dot = functools.partial(jnp.dot, preferred_element_type=F32)
 
         def body(tile, carry):
@@ -288,20 +293,31 @@
             value = dot(left_high, high) + (dot(left_high, low) + dot(left_low, high))
             part[panel, 2 * tile] = value[:half]
             part[panel, 2 * tile + 1] = value[half:]
+            wanted = row.mine == 1 - panel
+            if panel == 0:
+                wanted = wanted & ((tile > 0) | (col.place == 0))
+
+            @pl.when(wanted)
+            def _():
+                leaf_copy(panel, 2 * tile).start()
+                leaf_copy(panel, 2 * tile + 1).start()
+
+            between(tile)
             return carry
 
-        lax.fori_loop(first_slot // 2, SLOTS // 2, body, 0)
-
-        @pl.when(row.mine == 1 - panel)
-        def _():
-            send_start = jnp.where((col.place == 0) & (panel == 0), 0, 2)
-            loop(
-                send_start, SLOTS,
-                lambda s: remote(
-                    part.at[panel, s], from_partner.at[s], leaf_send.at[s], partner_recv.at[s],
-                    row, row.partner,
-                ).start(),
-            )
+        lax.fori_loop(first_tile, SLOTS // 2, body, 0)
+
+    def pass_rows(chunk):
+        @pl.when((chunk < ROW_CHUNKS) & jnp.logical_not(row.first))
+        def _():
+            pass_on(row, rows_buf, rows_size, chunk, rows_recv, rows_send)
+
+    def between_one(tile):
+        @pl.when((tile < CORNER_CHUNKS) & jnp.logical_not(top_row))
+        def _():
+            corner_step(tile)
+
+        pass_rows(tile)
 
     offdiag[0] = product(cols[0], inverse[0])
 
@@ -309,19 +325,15 @@
     def _():
         offdiag[0, :width] = jnp.zeros((width, width), F32)
 
-    own_terms(0, 0)
-
-    @pl.when(jnp.logical_not(top_row))
-    def _():
-        loop(0, CORNER_CHUNKS, corner_step)
-
+    own_terms(0, 0, between_one)
     offdiag[1] = product(cols[1] - product(offdiag[0], corner[...]), inverse[1])
 
     @pl.when(top_row)
     def _():
         offdiag[1, :width] = jnp.zeros((width, width), F32)
 
-    own_terms(1, 2)
+    own_terms(1, 1, lambda tile: pass_rows(SLOTS // 2 - 1 + tile))
+    loop(SLOTS - 1, ROW_CHUNKS, pass_rows)
 
     @pl.when(end_row)
     def _():
@@ -349,16 +361,7 @@
                 mine, from_next.at[slot], chain_send.at[slot], next_recv.at[slot], row, row.prev
             ).start()
 
-    def stream_step(index):
-        @pl.when((index < ROW_CHUNKS) & jnp.logical_not(row.first))
-        def _():
-            pass_on(row, rows_buf, rows_size, index, rows_recv, rows_send)
-
-        @pl.when(index >= slot_start)
-        def _():
-            reduce_step(index)
-
-    loop(0, 4, stream_step)
+    loop(slot_start, 4, reduce_step)
     crit_size = width // CRIT_CHUNKS
 
     @pl.when(end_row)
@@ -388,7 +391,7 @@
         offdiag[1, :width] = edge_own[...]
         dmat[...] = sym
 
-    loop(4, SLOTS, stream_step)
+    loop(4, SLOTS, reduce_step)
     loop(0, ROW_CHUNKS, lambda c: take(row, rows_buf, rows_size, c, rows_recv, rows_send))
 
     outs = [
@@ -463,13 +466,7 @@
 
     loop(0, CORNER_CHUNKS, corner_finish)
     leaf_start = jnp.where((col.place == 0) & (row.mine == 1), 0, 2)
-    loop(
-        leaf_start, SLOTS,
-        lambda s: remote(
-            part.at[1 - row.mine, s], from_partner.at[s], leaf_send.at[s], partner_recv.at[s],
-            row, row.partner,
-        ).wait_send(),
-    )
+    loop(leaf_start, SLOTS, lambda s: leaf_copy(1 - row.mine, s).wait_send())
 
     @pl.when(jnp.logical_not(row.first))
     def _():
@@ -588,7 +585,7 @@
             dma((2,)),
         ],
         compiler_params=pltpu.CompilerParams(
-            collective_id=0, has_side_effects=True, vmem_limit_bytes=40 * 2**20
+            collective_id=0, has_side_effects=True, vmem_limit_bytes=60 * 2**20
         ),
         name="panels",
     )(factor, adjoint, inverse)
@@ -606,7 +603,7 @@
             pl.BlockSpec((width, width), lambda t: (0, 0)),
         ],
         out_specs=pl.BlockSpec((width, total), lambda t: (t, 0)),
-        compiler_params=pltpu.CompilerParams(vmem_limit_bytes=40 * 2**20),
+        compiler_params=pltpu.CompilerParams(vmem_limit_bytes=60 * 2**20),
         name="update",
     )(adjoint, offdiag, rows, fix, phi)
 

time: 178 us -> 113 us (0.63)
  the two profiles are of different devices: /device:TPU:0 before, /device:TPU:31 now
where the time goes in v3:
time: 113 us; the launch traced here: 112 us
  Pallas kernels  112 us (99%)
    pallas_call x1, Pallas kernels, per_device(): pl.pallas_call(row_kernel, out_shape=[jax.ShapeDtypeStruct((2, top, width...  102 us
    pallas_call x1, Pallas kernels, per_device(): pl.pallas_call(update_kernel, grid=(steps,), out_shape=jax.ShapeDtypeStru...  9.84 us

profile of v3, /device:TPU:31, one launch (start us, length us, event | category | flops | bytes accessed | tf_op | source)
XLA Modules:
  0.0 112.3 jit_solution(10911738379202719637)
XLA Ops:
  0.0 102.5 %panels.1 = (f32[2,512,256]{2,1,0:T(8,128)}, f32[2,256,1024]{2,1,0:T(8,128)}, f32[256,1024]{1,0:T(8,128)}, f32[256,256]{1,0:T(8,128)}) custom-call(f32[1024,2048]{1,0:T(8,128)} %factor.1, f32[1024,2048]{1,0:T(8,128)} %adjoint.3, f32[2,256,256]{2,1,0:T(8,128)} %inverse.1), custom_call_target="tpu_custom_call" | custom-call | tf_op jit(solution)/shard_map/panels/pallas_call | solution.py:544
  102.5 9.8 %update.1 = f32[1024,2048]{1,0:T(8,128)} custom-call(f32[1024,2048]{1,0:T(8,128)} %adjoint.3, f32[2,512,256]{2,1,0:T(8,128)} %get-tuple-element.9.offdiag, f32[2,256,1024]{2,1,0:T(8,128)} %get-tuple-element.10.rows, f32[256,1024]{1,0:T(8,128)} %get-tuple-element.11.fix, f32[256,256]{1,0:T(8,128)} %get-tuple-element.12.phi), custom_call_target="tpu_custom_call" | custom-call | tf_op jit(solution)/shard_map/update/pallas_call | solution.py:594

commit v4 on v3

--- a/solution.py
+++ b/solution.py
@@ -13,6 +13,7 @@
 COL_CHUNKS = 4
 CORNER_CHUNKS = 4
 ROW_CHUNKS = 8
+EARLY_CHUNKS = 4
 CRIT_CHUNKS = 2
 
 
@@ -265,13 +266,18 @@
 
         corner_rows(chunk)
 
+    def send_rows(start, stop):
+        @pl.when(row.first)
+        def _():
+            loop(start, stop, lambda c: pass_on(row, rows_buf, rows_size, c, rows_recv, rows_send))
+
+    send_rows(0, EARLY_CHUNKS)
+
     @pl.when(top_row)
     def _():
         loop(0, CORNER_CHUNKS, corner_step)
 
-    @pl.when(row.first)
-    def _():
-        loop(0, ROW_CHUNKS, lambda c: pass_on(row, rows_buf, rows_size, c, rows_recv, rows_send))
+    send_rows(EARLY_CHUNKS, ROW_CHUNKS)
 
     loop(0, COL_CHUNKS, lambda c: take(col, cols, cols_size, c, cols_recv, cols_send))
     lower_load.wait()
@@ -313,31 +319,13 @@
             pass_on(row, rows_buf, rows_size, chunk, rows_recv, rows_send)
 
     def between_one(tile):
-        @pl.when((tile < CORNER_CHUNKS) & jnp.logical_not(top_row))
-        def _():
-            corner_step(tile)
-
-        pass_rows(tile)
-
-    offdiag[0] = product(cols[0], inverse[0])
-
-    @pl.when(top_row)
-    def _():
-        offdiag[0, :width] = jnp.zeros((width, width), F32)
-
-    own_terms(0, 0, between_one)
-    offdiag[1] = product(cols[1] - product(offdiag[0], corner[...]), inverse[1])
-
-    @pl.when(top_row)
-    def _():
-        offdiag[1, :width] = jnp.zeros((width, width), F32)
-
-    own_terms(1, 1, lambda tile: pass_rows(SLOTS // 2 - 1 + tile))
-    loop(SLOTS - 1, ROW_CHUNKS, pass_rows)
-
-    @pl.when(end_row)
-    def _():
-        dmat[...] = lower_inverse(inverse[row.mine])
+        @pl.when(tile < EARLY_CHUNKS)
+        def _():
+            pass_rows(tile)
+
+        @pl.when((tile == SLOTS // 2 - 1) & jnp.logical_not(top_row))
+        def _():
+            loop(0, CORNER_CHUNKS, corner_step)
 
     slot_start = jnp.where((col.place == 0) & (row.mine == 0), 0, 2)
 
@@ -361,7 +349,34 @@
                 mine, from_next.at[slot], chain_send.at[slot], next_recv.at[slot], row, row.prev
             ).start()
 
-    loop(slot_start, 4, reduce_step)
+    offdiag[0] = product(cols[0], inverse[0])
+
+    @pl.when(top_row)
+    def _():
+        offdiag[0, :width] = jnp.zeros((width, width), F32)
+
+    own_terms(0, 0, between_one)
+
+    early_sums = (row.mine == 0) & jnp.logical_not(row.first)
+
+    @pl.when(early_sums)
+    def _():
+        loop(slot_start, 4, reduce_step)
+
+    offdiag[1] = product(cols[1] - product(offdiag[0], corner[...]), inverse[1])
+
+    @pl.when(top_row)
+    def _():
+        offdiag[1, :width] = jnp.zeros((width, width), F32)
+
+    own_terms(1, 1, lambda tile: pass_rows(EARLY_CHUNKS - 1 + tile))
+    loop(EARLY_CHUNKS + SLOTS // 2 - 1, ROW_CHUNKS, pass_rows)
+
+    @pl.when(end_row)
+    def _():
+        dmat[...] = lower_inverse(inverse[row.mine])
+
+    loop(jnp.where(early_sums, 4, slot_start), 4, reduce_step)
     crit_size = width // CRIT_CHUNKS
 
     @pl.when(end_row)

time: 113 us -> 112 us (level)
  the two profiles are of different devices: /device:TPU:31 before, /device:TPU:0 now
where the time goes in v4:
time: 112 us; the launch traced here: 110 us
  Pallas kernels  110 us (98%)
    pallas_call x1, Pallas kernels, per_device(): pl.pallas_call(row_kernel, out_shape=[jax.ShapeDtypeStruct((2, top, width...  100 us
    pallas_call x1, Pallas kernels, per_device(): pl.pallas_call(update_kernel, grid=(steps,), out_shape=jax.ShapeDtypeStru...  9.95 us

profile of v4, /device:TPU:0, one launch (start us, length us, event | category | flops | bytes accessed | tf_op | source)
XLA Modules:
  0.0 110.0 jit_solution(7456677205074529468)
XLA Ops:
  0.0 100.1 %panels.1 = (f32[2,512,256]{2,1,0:T(8,128)}, f32[2,256,1024]{2,1,0:T(8,128)}, f32[256,1024]{1,0:T(8,128)}, f32[256,256]{1,0:T(8,128)}) custom-call(f32[1024,2048]{1,0:T(8,128)} %factor.1, f32[1024,2048]{1,0:T(8,128)} %adjoint.3, f32[2,256,256]{2,1,0:T(8,128)} %inverse.1), custom_call_target="tpu_custom_call" | custom-call | tf_op jit(solution)/shard_map/panels/pallas_call | solution.py:559
  100.1 9.9 %update.1 = f32[1024,2048]{1,0:T(8,128)} custom-call(f32[1024,2048]{1,0:T(8,128)} %adjoint.3, f32[2,512,256]{2,1,0:T(8,128)} %get-tuple-element.9.offdiag, f32[2,256,1024]{2,1,0:T(8,128)} %get-tuple-element.10.rows, f32[256,1024]{1,0:T(8,128)} %get-tuple-element.11.fix, f32[256,256]{1,0:T(8,128)} %get-tuple-element.12.phi), custom_call_target="tpu_custom_call" | custom-call | tf_op jit(solution)/shard_map/update/pallas_call | solution.py:609

commit v5 on v4

--- a/solution.py
+++ b/solution.py
@@ -84,7 +84,7 @@
     lower, cols, offdiag, rows_buf, corner, part, from_partner, from_next, crit, ldiag,
     edge_in, edge_own, dmat, local_sem, load_sem,
     cols_recv, cols_send, corner_crecv, corner_csend, corner_rrecv, corner_rsend,
-    rows_recv, rows_send, leaf_send, chain_send, partner_recv, next_recv,
+    rows_recv, rows_send, back_send, leaf_send, chain_send, partner_recv, next_recv,
     crit_recv, crit_send, edge_sems, out_sem,
 ):
     width = inverse.shape[-1]
@@ -266,10 +266,43 @@
 
         corner_rows(chunk)
 
+    def rows_ref(panel, chunk):
+        return rows_buf.at[panel, pl.ds(pl.multiple_of(chunk * rows_size, 8), rows_size)]
+
+    def rows_copy(panel, chunk, send, target):
+        ref = rows_ref(panel, chunk)
+        return remote(ref, ref, send, rows_recv.at[panel, chunk], row, target)
+
+    def rows_next(chunk):
+        return rows_copy(row.mine, chunk, rows_send.at[0, chunk], row.next)
+
+    def rows_partner(chunk):
+        return rows_copy(row.mine, chunk, rows_send.at[1, chunk], row.partner)
+
+    def rows_back(chunk):
+        return rows_copy(1 - row.mine, chunk, back_send.at[chunk], row.prev)
+
+    def pass_rows(chunk):
+        @pl.when(jnp.logical_not(row.first))
+        def _():
+            rows_next(chunk).wait_recv()
+
+        @pl.when(jnp.logical_not(row.last))
+        def _():
+            rows_next(chunk).start()
+
+        @pl.when(row.first | (chunk < EARLY_CHUNKS))
+        def _():
+            rows_partner(chunk).start()
+
+    def pass_back(chunk):
+        rows_back(chunk).wait_recv()
+        rows_back(chunk).start()
+
     def send_rows(start, stop):
         @pl.when(row.first)
         def _():
-            loop(start, stop, lambda c: pass_on(row, rows_buf, rows_size, c, rows_recv, rows_send))
+            loop(start, stop, pass_rows)
 
     send_rows(0, EARLY_CHUNKS)
 
@@ -313,15 +346,11 @@
 
         lax.fori_loop(first_tile, SLOTS // 2, body, 0)
 
-    def pass_rows(chunk):
-        @pl.when((chunk < ROW_CHUNKS) & jnp.logical_not(row.first))
-        def _():
-            pass_on(row, rows_buf, rows_size, chunk, rows_recv, rows_send)
-
     def between_one(tile):
-        @pl.when(tile < EARLY_CHUNKS)
-        def _():
-            pass_rows(tile)
+        @pl.when((tile < SLOTS // 2 - 1) & jnp.logical_not(row.first))
+        def _():
+            pass_rows(2 * tile)
+            pass_rows(2 * tile + 1)
 
         @pl.when((tile == SLOTS // 2 - 1) & jnp.logical_not(top_row))
         def _():
@@ -369,8 +398,11 @@
     def _():
         offdiag[1, :width] = jnp.zeros((width, width), F32)
 
-    own_terms(1, 1, lambda tile: pass_rows(EARLY_CHUNKS - 1 + tile))
-    loop(EARLY_CHUNKS + SLOTS // 2 - 1, ROW_CHUNKS, pass_rows)
+    own_terms(1, 1, lambda tile: None)
+
+    @pl.when(jnp.logical_not(row.first))
+    def _():
+        loop(EARLY_CHUNKS, ROW_CHUNKS, pass_back)
 
     @pl.when(end_row)
     def _():
@@ -407,7 +439,10 @@
         dmat[...] = sym
 
     loop(4, SLOTS, reduce_step)
-    loop(0, ROW_CHUNKS, lambda c: take(row, rows_buf, rows_size, c, rows_recv, rows_send))
+    loop(
+        0, jnp.where(row.first, ROW_CHUNKS, EARLY_CHUNKS),
+        lambda c: rows_copy(1 - row.mine, c, rows_send.at[1, c], row.partner).wait_recv(),
+    )
 
     outs = [
         pltpu.make_async_copy(offdiag, a_out, out_sem.at[0]),
@@ -446,7 +481,21 @@
         lax.fori_loop(0, side // width, body, 0)
 
     finish_sends(col, cols, cols_size, COL_CHUNKS, cols_send, cols_recv)
-    finish_sends(row, rows_buf, rows_size, ROW_CHUNKS, rows_send, rows_recv)
+
+    def rows_finish(chunk):
+        @pl.when(jnp.logical_not(row.last))
+        def _():
+            rows_next(chunk).wait_send()
+
+        @pl.when(row.first | (chunk < EARLY_CHUNKS))
+        def _():
+            rows_partner(chunk).wait_send()
+
+        @pl.when(jnp.logical_not(row.first) & (chunk >= EARLY_CHUNKS))
+        def _():
+            rows_back(chunk).wait_send()
+
+    loop(0, ROW_CHUNKS, rows_finish)
 
     @pl.when(end_row)
     def _():
@@ -501,7 +550,7 @@
         copy.wait()
 
 
-def update_kernel(adjoint, offdiag, rows, fix, phi, out):
+def update_kernel(adjoint, offdiag, rows, fix, phi, out, high, low):
     step = pl.program_id(0)
     middle = pl.num_programs(0) // 2
     width, side = phi.shape[0], fix.shape[1]
@@ -511,17 +560,24 @@
     last_col = lax.axis_index("col") == lax.axis_size("col") - 1
     out[...] = adjoint[...]
 
+    for panel in range(2):
+
+        @pl.when(step == panel)
+        def _():
+            span = slice(panel * width, (panel + 1) * width)
+            high[span], low[span] = split(rows[panel])
+
     @pl.when(step >= middle)
     def _():
-        pairs = [split(offdiag[panel]) for panel in range(2)]
+        left_high, left_low = split(jnp.concatenate([offdiag[0], offdiag[1]], axis=1))
         dot = functools.partial(jnp.dot, preferred_element_type=F32)
 
         for start in range(0, side, width):
-            value = adjoint[:, start : start + width]
-            for panel, (left_high, left_low) in enumerate(pairs):
-                high, low = split(rows[panel, :, start : start + width])
-                value -= dot(left_high, high) + (dot(left_high, low) + dot(left_low, high))
-            out[:, start : start + width] = value
+            span = slice(start, start + width)
+            out[:, span] = adjoint[:, span] - (
+                dot(left_high, high[:, span])
+                + (dot(left_high, low[:, span]) + dot(left_low, high[:, span]))
+            )
 
         @pl.when(top_row & (step == middle))
         def _():
@@ -590,6 +646,7 @@
             dma((2, CORNER_CHUNKS)),
             dma((2, ROW_CHUNKS)),
             dma((2, ROW_CHUNKS)),
+            dma((ROW_CHUNKS,)),
             dma((SLOTS,)),
             dma((SLOTS,)),
             dma((SLOTS,)),
@@ -618,6 +675,7 @@
             pl.BlockSpec((width, width), lambda t: (0, 0)),
         ],
         out_specs=pl.BlockSpec((width, total), lambda t: (t, 0)),
+        scratch_shapes=[pltpu.VMEM((2 * width, side), jnp.bfloat16)] * 2,
         compiler_params=pltpu.CompilerParams(vmem_limit_bytes=60 * 2**20),
         name="update",
     )(adjoint, offdiag, rows, fix, phi)

time: 112 us -> 114 us (1.018)
  Pallas kernels: 110 us -> 113 us
    pallas_call x1, Pallas kernels: 100 us -> 103 us  [per_device(): pl.pallas_call(row_kernel, out_shape=[jax.ShapeDtypeStruct((2, top, width...]
where the time goes in v5:
time: 114 us; the launch traced here: 113 us
  Pallas kernels  113 us (99%)
    pallas_call x1, Pallas kernels, per_device(): pl.pallas_call(row_kernel, out_shape=[jax.ShapeDtypeStruct((2, top, width...  103 us
    pallas_call x1, Pallas kernels, per_device(): pl.pallas_call(update_kernel, grid=(steps,), out_shape=jax.ShapeDtypeStru...  10.1 us

profile of v5, /device:TPU:0, one launch (start us, length us, event | category | flops | bytes accessed | tf_op | source)
XLA Modules:
  0.0 112.7 jit_solution(3474892491339048183)
XLA Ops:
  0.0 102.6 %panels.1 = (f32[2,512,256]{2,1,0:T(8,128)}, f32[2,256,1024]{2,1,0:T(8,128)}, f32[256,1024]{1,0:T(8,128)}, f32[256,256]{1,0:T(8,128)}) custom-call(f32[1024,2048]{1,0:T(8,128)} %factor.1, f32[1024,2048]{1,0:T(8,128)} %adjoint.3, f32[2,256,256]{2,1,0:T(8,128)} %inverse.1), custom_call_target="tpu_custom_call" | custom-call | tf_op jit(solution)/shard_map/panels/pallas_call | solution.py:615
  102.6 10.1 %update.1 = f32[1024,2048]{1,0:T(8,128)} custom-call(f32[1024,2048]{1,0:T(8,128)} %adjoint.3, f32[2,512,256]{2,1,0:T(8,128)} %get-tuple-element.9.offdiag, f32[2,256,1024]{2,1,0:T(8,128)} %get-tuple-element.10.rows, f32[256,1024]{1,0:T(8,128)} %get-tuple-element.11.fix, f32[256,256]{1,0:T(8,128)} %get-tuple-element.12.phi), custom_call_target="tpu_custom_call" | custom-call | tf_op jit(solution)/shard_map/update/pallas_call | solution.py:666

commit v6 on v4

--- a/solution.py
+++ b/solution.py
@@ -13,7 +13,7 @@
 COL_CHUNKS = 4
 CORNER_CHUNKS = 4
 ROW_CHUNKS = 8
-EARLY_CHUNKS = 4
+EARLY_CHUNKS = 2
 CRIT_CHUNKS = 2
 
 
@@ -206,7 +206,6 @@
     cols_size = top // COL_CHUNKS
     rows_size = width // ROW_CHUNKS
     corner_size = width // CORNER_CHUNKS
-    loop(0, COL_CHUNKS, lambda c: pass_on(col, cols, cols_size, c, cols_recv, cols_send))
 
     def corner_ref(chunk):
         return corner.at[pl.ds(pl.multiple_of(chunk * corner_size, 8), corner_size)]
@@ -238,6 +237,12 @@
                 ref, ref, corner_csend.at[1, chunk], corner_crecv.at[chunk], col, col.partner
             ).wait_recv()
 
+    @pl.when(top_row & (col.place == col.count - 1))
+    def _():
+        loop(0, CORNER_CHUNKS, corner_cols)
+
+    loop(0, COL_CHUNKS, lambda c: pass_on(col, cols, cols_size, c, cols_recv, cols_send))
+
     def corner_rows(chunk):
         ref = corner_ref(chunk)
 
@@ -260,7 +265,7 @@
             ).start()
 
     def corner_step(chunk):
-        @pl.when(top_row)
+        @pl.when(top_row & jnp.logical_not(col.place == col.count - 1))
         def _():
             corner_cols(chunk)
 
@@ -319,13 +324,11 @@
             pass_on(row, rows_buf, rows_size, chunk, rows_recv, rows_send)
 
     def between_one(tile):
-        @pl.when(tile < EARLY_CHUNKS)
-        def _():
-            pass_rows(tile)
-
-        @pl.when((tile == SLOTS // 2 - 1) & jnp.logical_not(top_row))
+        @pl.when((tile == EARLY_CHUNKS) & jnp.logical_not(top_row))
         def _():
             loop(0, CORNER_CHUNKS, corner_step)
+
+        pass_rows(tile)
 
     slot_start = jnp.where((col.place == 0) & (row.mine == 0), 0, 2)
 
@@ -357,26 +360,20 @@
 
     own_terms(0, 0, between_one)
 
-    early_sums = (row.mine == 0) & jnp.logical_not(row.first)
-
-    @pl.when(early_sums)
-    def _():
-        loop(slot_start, 4, reduce_step)
-
     offdiag[1] = product(cols[1] - product(offdiag[0], corner[...]), inverse[1])
 
     @pl.when(top_row)
     def _():
         offdiag[1, :width] = jnp.zeros((width, width), F32)
 
-    own_terms(1, 1, lambda tile: pass_rows(EARLY_CHUNKS - 1 + tile))
-    loop(EARLY_CHUNKS + SLOTS // 2 - 1, ROW_CHUNKS, pass_rows)
+    own_terms(1, 1, lambda tile: pass_rows(SLOTS // 2 - 1 + tile))
+    loop(SLOTS - 1, ROW_CHUNKS, pass_rows)
 
     @pl.when(end_row)
     def _():
         dmat[...] = lower_inverse(inverse[row.mine])
 
-    loop(jnp.where(early_sums, 4, slot_start), 4, reduce_step)
+    loop(slot_start, 4, reduce_step)
     crit_size = width // CRIT_CHUNKS
 
     @pl.when(end_row)

time: 112 us -> 108 us (0.964)
  the two profiles are of different devices: /device:TPU:0 before, /device:TPU:31 now
where the time goes in v6:
time: 108 us
  Pallas kernels  108 us (100%)
    pallas_call x1, Pallas kernels, per_device(): pl.pallas_call(row_kernel, out_shape=[jax.ShapeDtypeStruct((2, top, width...  98.1 us
    pallas_call x1, Pallas kernels, per_device(): pl.pallas_call(update_kernel, grid=(steps,), out_shape=jax.ShapeDtypeStru...  9.84 us

profile of v6, /device:TPU:31, one launch (start us, length us, event | category | flops | bytes accessed | tf_op | source)
XLA Modules:
  0.0 108.0 jit_solution(10807751399257273677)
XLA Ops:
  0.0 98.1 %panels.1 = (f32[2,512,256]{2,1,0:T(8,128)}, f32[2,256,1024]{2,1,0:T(8,128)}, f32[256,1024]{1,0:T(8,128)}, f32[256,256]{1,0:T(8,128)}) custom-call(f32[1024,2048]{1,0:T(8,128)} %factor.1, f32[1024,2048]{1,0:T(8,128)} %adjoint.3, f32[2,256,256]{2,1,0:T(8,128)} %inverse.1), custom_call_target="tpu_custom_call" | custom-call | tf_op jit(solution)/shard_map/panels/pallas_call | solution.py:556
  98.1 9.8 %update.1 = f32[1024,2048]{1,0:T(8,128)} custom-call(f32[1024,2048]{1,0:T(8,128)} %adjoint.3, f32[2,512,256]{2,1,0:T(8,128)} %get-tuple-element.9.offdiag, f32[2,256,1024]{2,1,0:T(8,128)} %get-tuple-element.10.rows, f32[256,1024]{1,0:T(8,128)} %get-tuple-element.11.fix, f32[256,256]{1,0:T(8,128)} %get-tuple-element.12.phi), custom_call_target="tpu_custom_call" | custom-call | tf_op jit(solution)/shard_map/update/pallas_call | solution.py:606

commit v7 on v6

--- a/solution.py
+++ b/solution.py
@@ -241,7 +241,12 @@
     def _():
         loop(0, CORNER_CHUNKS, corner_cols)
 
-    loop(0, COL_CHUNKS, lambda c: pass_on(col, cols, cols_size, c, cols_recv, cols_send))
+    def pass_cols():
+        loop(0, COL_CHUNKS, lambda c: pass_on(col, cols, cols_size, c, cols_recv, cols_send))
+
+    @pl.when(col.first)
+    def _():
+        pass_cols()
 
     def corner_rows(chunk):
         ref = corner_ref(chunk)
@@ -281,6 +286,10 @@
     @pl.when(top_row)
     def _():
         loop(0, CORNER_CHUNKS, corner_step)
+
+    @pl.when(jnp.logical_not(col.first))
+    def _():
+        pass_cols()
 
     send_rows(EARLY_CHUNKS, ROW_CHUNKS)
 

time: 108 us -> 103 us (0.954)
  the two profiles are of different devices: /device:TPU:31 before, /device:TPU:30 now
where the time goes in v7:
time: 103 us
  Pallas kernels  103 us (100%)
    pallas_call x1, Pallas kernels, per_device(): pl.pallas_call(row_kernel, out_shape=[jax.ShapeDtypeStruct((2, top, width...  93.1 us
    pallas_call x1, Pallas kernels, per_device(): pl.pallas_call(update_kernel, grid=(steps,), out_shape=jax.ShapeDtypeStru...  9.81 us

profile of v7, /device:TPU:30, one launch (start us, length us, event | category | flops | bytes accessed | tf_op | source)
XLA Modules:
  0.0 102.9 jit_solution(17441985075724118881)
XLA Ops:
  0.0 93.1 %panels.1 = (f32[2,512,256]{2,1,0:T(8,128)}, f32[2,256,1024]{2,1,0:T(8,128)}, f32[256,1024]{1,0:T(8,128)}, f32[256,256]{1,0:T(8,128)}) custom-call(f32[1024,2048]{1,0:T(8,128)} %factor.1, f32[1024,2048]{1,0:T(8,128)} %adjoint.3, f32[2,256,256]{2,1,0:T(8,128)} %inverse.1), custom_call_target="tpu_custom_call" | custom-call | tf_op jit(solution)/shard_map/panels/pallas_call | solution.py:565
  93.1 9.8 %update.1 = f32[1024,2048]{1,0:T(8,128)} custom-call(f32[1024,2048]{1,0:T(8,128)} %adjoint.3, f32[2,512,256]{2,1,0:T(8,128)} %get-tuple-element.9.offdiag, f32[2,256,1024]{2,1,0:T(8,128)} %get-tuple-element.10.rows, f32[256,1024]{1,0:T(8,128)} %get-tuple-element.11.fix, f32[256,256]{1,0:T(8,128)} %get-tuple-element.12.phi), custom_call_target="tpu_custom_call" | custom-call | tf_op jit(solution)/shard_map/update/pallas_call | solution.py:615
